TPU v7x, 256 devices: a whole 4x4x8 slice. The times are simulated.
256 devices in a mesh: path: 8 (over z), tm: 32 (over x, y, core).
Axes of the slice: x: 4, y: 4, z: 8, core: 2. Of those that a mesh axis runs over, the one named last changes fastest.
Arguments:
- values: bfloat16 [4096, 64, 2048], P('path', 'tm'), may hold values from -5 to 5
- hazard: float32 [64, 4096], P('tm', 'path'), may hold values from 0.003125 to 0.046875
- spread: float32 [64], P('tm'), may hold values from 0.3 to 3
- trade_set: int32 [2048], replicated, may hold values from 0 to 255
Outputs:
- pathwise_fva: float32 [4096, 256], P(('path', 'tm'))
- set_fva: float32 [256], P(('path', 'tm'))
All inputs are finite; a program needn't handle non-finite values.
Results may differ from a plain program's by a relative error of at most 0.0003.
Values sent between devices are 32-bit elements; how exact they have to be, the bound alone decides.
No kernel may reach another device: no remote copies, remote signals or barrier semaphores. Data moves between devices by JAX's collectives and lax.ppermute only.
A program may use at most 64 MiB of HBM per device.

v0:
```python
import jax
import jax.numpy as jnp
from jax import lax
from jax.experimental import pallas as pl
from jax.experimental.pallas import tpu as pltpu
from jax.sharding import Mesh
from jax.sharding import PartitionSpec as P

SETS = 256
LANES = 128
ROWS = 128
XY = 16
DATES = 64
PATHS = 4096
MESSAGE = 68
FAR = 10
MIB = 2**20
VMEM = pl.BlockSpec(memory_space=pltpu.VMEM)
ANY = pl.BlockSpec(memory_space=pl.ANY)
HALF_ROWS = XY * 32
HALF = jax.ShapeDtypeStruct((HALF_ROWS + 8, LANES), jnp.float32)


def columns(row):
    return jnp.transpose(jnp.broadcast_to(row, (LANES, LANES)))


def in_hbm(array):
    return pltpu.with_memory_space_constraint(array, pltpu.HBM)


def net_kernel(
    values_hbm,
    hazard_hbm,
    spread_hbm,
    set_hbm,
    keep_ref,
    give_ref,
    values_ref,
    hazard_ref,
    spread_ref,
    set_ref,
    net_ref,
    hot_ref,
    both_ref,
    own_ref,
    sem,
):
    half_paths = values_hbm.shape[0] // 2
    small = [
        pltpu.make_async_copy(set_hbm, set_ref, sem.at[0]),
        pltpu.make_async_copy(hazard_hbm, hazard_ref, sem.at[1]),
        pltpu.make_async_copy(spread_hbm, spread_ref, sem.at[2]),
    ]
    large = [
        pltpu.make_async_copy(
            values_hbm.at[pl.ds(part * half_paths, half_paths)],
            values_ref.at[pl.ds(part * half_paths, half_paths)],
            sem.at[3 + part],
        )
        for part in range(2)
    ]
    for copy in small + large:
        copy.start()
    for copy in small:
        copy.wait()
    lane = lax.broadcasted_iota(jnp.int32, (LANES, LANES), 1)
    for at in range(0, set_ref.shape[1], LANES):
        ids = columns(set_ref[:, at : at + LANES])
        for half in range(2):
            hot_ref[at : at + LANES, half * LANES : (half + 1) * LANES] = jnp.where(
                ids == lane + half * LANES, 1.0, 0.0
            ).astype(jnp.bfloat16)
    core = lax.axis_index("c")
    own = hazard_ref[0:1, :] + hazard_ref[1:2, :]
    before = jnp.where(core == 0, 0.0, own)
    weight_0 = spread_ref[:, 0:1] * jnp.exp(hazard_ref[1:2, :] - before)
    weight_1 = jnp.broadcast_to(spread_ref[:, 1:2], own.shape) * jnp.exp(-before)
    for at in range(0, own.shape[1], LANES):
        own_ref[at : at + LANES, :] = columns(own[:, at : at + LANES])
    for out_ref, parity in ((keep_ref, core), (give_ref, 1 - core)):
        for part in range(2):
            kept = [
                own_ref[pl.ds(pl.multiple_of((2 * i + parity) * 16, 16), 16), :]
                for i in range(part * 8, part * 8 + 8)
            ]
            row = jnp.transpose(jnp.concatenate(kept, axis=0))[0:1, :]
            out_ref[HALF_ROWS + part * 4 : HALF_ROWS + part * 4 + 4, :] = jnp.broadcast_to(
                row, (4, LANES)
            )
    for at in range(0, values_ref.shape[0], ROWS):
        if at % half_paths == 0:
            large[at // half_paths].wait()
        block = values_ref[at : at + ROWS].reshape(2 * ROWS, values_ref.shape[2])
        netted = jnp.dot(block, hot_ref[...], preferred_element_type=jnp.float32)
        column_0 = columns(weight_0[:, at : at + ROWS])
        column_1 = columns(weight_1[:, at : at + ROWS])
        for half in range(2):
            net_ref[half, 2 * at : 2 * at + 2 * ROWS] = netted[
                :, half * LANES : (half + 1) * LANES
            ]
            even = net_ref[half, pl.ds(2 * at, ROWS, 2), :]
            odd = net_ref[half, pl.ds(2 * at + 1, ROWS, 2), :]
            funded = column_0 * jnp.maximum(even, 0.0) + column_1 * jnp.maximum(odd, 0.0)
            for j in range(ROWS // 16):
                block_at = at // 16 + j
                row_at = block_at // 2 * 32 + half * 16
                both_ref[block_at % 2, row_at : row_at + 16, :] = funded[j * 16 : j * 16 + 16, :]
    for out_ref, parity in ((keep_ref, core), (give_ref, 1 - core)):
        out_ref[0:HALF_ROWS, :] = both_ref[parity]


def local_sums(values, hazard, spread, trade_set):
    paths, dates, trades = values.shape
    return pl.pallas_call(
        net_kernel,
        out_shape=(HALF, HALF),
        in_specs=[ANY, ANY, ANY, ANY],
        out_specs=(VMEM, VMEM),
        scratch_shapes=[
            pltpu.VMEM(values.shape, values.dtype),
            pltpu.VMEM(hazard.shape, hazard.dtype),
            pltpu.VMEM((1, dates), jnp.float32),
            pltpu.VMEM((1, trades), jnp.int32),
            pltpu.VMEM((2, paths * dates + 8, LANES), jnp.float32),
            pltpu.VMEM((trades, SETS), jnp.bfloat16),
            pltpu.VMEM((2, HALF_ROWS, LANES), jnp.float32),
            pltpu.VMEM((paths, LANES), jnp.float32),
            pltpu.SemaphoreType.DMA((5,)),
        ],
        compiler_params=pltpu.CompilerParams(vmem_limit_bytes=16 * MIB),
        cost_estimate=pl.CostEstimate(
            flops=2 * paths * dates * trades * SETS, bytes_accessed=5 * MIB, transcendentals=1024
        ),
        name="local_sums",
    )(in_hbm(values), in_hbm(hazard), in_hbm(spread[None, :]), in_hbm(trade_set[None, :]))


def pack_kernel(keep_ref, got_ref, out_ref, turned_ref):
    rows_ref = out_ref.reshape(XY * MESSAGE, LANES)
    core = lax.axis_index("c")
    for part in range(2):
        halves = [[], []]
        for i in range(part * 8, part * 8 + 8):
            for half in range(2):
                rows = slice(i * 32 + half * 16, i * 32 + half * 16 + 16)
                both = keep_ref[rows, :] + got_ref[rows, :]
                rows_ref[(i ^ FAR) * MESSAGE + half * 16 : (i ^ FAR) * MESSAGE + half * 16 + 16, :] = both
                halves[half].append(both)
        for half in range(2):
            turned_ref[part, half * LANES : (half + 1) * LANES, :] = jnp.transpose(
                jnp.concatenate(halves[half], axis=0)
            )
        row = slice(HALF_ROWS + part * 4, HALF_ROWS + part * 4 + 1)
        own, other = keep_ref[row, :], got_ref[row, :]
        first = jnp.where(core == 0, own, other)
        for i in range(XY):
            rows_ref[(i ^ FAR) * MESSAGE + 64 + part : (i ^ FAR) * MESSAGE + 65 + part, :] = first
            rows_ref[(i ^ FAR) * MESSAGE + 66 + part : (i ^ FAR) * MESSAGE + 67 + part, :] = own + other
            for owner in range(2):
                at = (i ^ FAR) * MESSAGE + 32 + part * 16 + owner * 8
                rows_ref[at : at + 8, :] = turned_ref[part, pl.ds(2 * i + owner, 8, 32), :]


def packed(keep, got):
    return pl.pallas_call(
        pack_kernel,
        out_shape=jax.ShapeDtypeStruct((XY, MESSAGE // 2, 2, LANES), jnp.float32),
        in_specs=[VMEM, VMEM],
        out_specs=VMEM,
        scratch_shapes=[pltpu.VMEM((2, SETS + 32, LANES), jnp.float32)],
        compiler_params=pltpu.CompilerParams(vmem_limit_bytes=4 * MIB),
        cost_estimate=pl.CostEstimate(flops=10**6, bytes_accessed=MIB, transcendentals=0),
        name="packed",
    )(keep, got)


def set_kernel(arrived_ref, earlier_ref, parts_ref):
    rows_ref = arrived_ref.reshape(XY * MESSAGE, LANES)
    prefix = jnp.zeros((2, LANES), jnp.float32)
    total = [jnp.zeros((16, LANES), jnp.float32)] * 2
    for k in range(XY):
        at = (k ^ FAR) * MESSAGE + 64
        earlier = jnp.exp(-(prefix + rows_ref[at : at + 2, :])) * (1.0 / DATES)
        prefix = prefix + rows_ref[at + 2 : at + 4, :]
        for part in range(2):
            row = earlier[part : part + 1, :]
            earlier_ref[part, k : k + 1, :] = row
            at = (k ^ FAR) * MESSAGE + 32 + part * 16
            total[part] = total[part] + row * rows_ref[at : at + 16, :]
    sums = jnp.sum(total[0] + total[1], axis=1, keepdims=True) * (1.0 / PATHS)
    sums = jnp.broadcast_to(sums, (16, LANES))
    order = [sums[4:8], sums[0:4], sums[12:16], sums[8:12]]
    parts_ref[...] = jnp.concatenate(order, axis=0)[:, None, :]


def set_parts(arrived):
    return pl.pallas_call(
        set_kernel,
        out_shape=(
            jax.ShapeDtypeStruct((2, XY, LANES), jnp.float32),
            jax.ShapeDtypeStruct((16, 1, LANES), jnp.float32),
        ),
        in_specs=[VMEM],
        out_specs=(VMEM, VMEM),
        compiler_params=pltpu.CompilerParams(vmem_limit_bytes=2 * MIB),
        cost_estimate=pl.CostEstimate(flops=10**6, bytes_accessed=2**19, transcendentals=4096),
        name="set_parts",
    )(arrived)


def last_kernel(arrived_ref, earlier_ref, parts_ref, paths_ref, set_ref, turned_ref):
    rows_ref = arrived_ref.reshape(XY * MESSAGE, LANES)
    chip = lax.axis_index("x") * 4 + lax.axis_index("y")
    padding = jnp.zeros((LANES - XY, LANES), jnp.float32)
    for part in range(2):
        turned_ref[part * LANES : (part + 1) * LANES, :] = jnp.transpose(
            jnp.concatenate([earlier_ref[part], padding], axis=0)
        )
    own = turned_ref[pl.ds(pl.multiple_of(chip * 16, 16), 16), :]
    total = [jnp.zeros((16, LANES), jnp.float32)] * 2
    for k in range(XY):
        weight = own[:, k : k + 1]
        for half in range(2):
            at = (k ^ FAR) * MESSAGE + half * 16
            total[half] = total[half] + weight * rows_ref[at : at + 16, :]
    for half in range(2):
        paths_ref[:, half * LANES : (half + 1) * LANES] = total[half]
    set_ref[...] = jnp.sum(parts_ref[...], axis=0)


def last_sums(arrived, earlier, parts):
    return pl.pallas_call(
        last_kernel,
        out_shape=(
            jax.ShapeDtypeStruct((16, SETS), jnp.float32),
            jax.ShapeDtypeStruct((1, LANES), jnp.float32),
        ),
        in_specs=[VMEM, VMEM, VMEM],
        out_specs=(VMEM, VMEM),
        scratch_shapes=[pltpu.VMEM((2 * LANES, LANES), jnp.float32)],
        compiler_params=pltpu.CompilerParams(vmem_limit_bytes=2 * MIB),
        cost_estimate=pl.CostEstimate(flops=10**6, bytes_accessed=2**19, transcendentals=0),
        name="last_sums",
    )(arrived, earlier, parts)


def on_device(values, hazard, spread, trade_set):
    keep, give = local_sums(values, hazard, spread, trade_set)
    got = lax.ppermute(give, "c", [(0, 1), (1, 0)])
    chips = [i ^ FAR for i in range(XY)]
    arrived = lax.all_to_all(
        packed(keep, got), ("x", "y"), 0, 0, tiled=True, axis_index_groups=[chips]
    )
    earlier, parts = set_parts(arrived)
    order = [core * 8 + (z + 4) % 8 for core in range(2) for z in range(8)]
    parts = lax.all_to_all(parts, ("c", "z"), 0, 0, tiled=True, axis_index_groups=[order])
    pathwise, sets = last_sums(arrived, earlier, parts)
    return pathwise, sets[0, 0:1]


def solution(mesh):
    split = Mesh(mesh.devices.reshape(mesh.shape["path"], 4, 4, 2), ("z", "x", "y", "c"))
    tm = ("x", "y", "c")
    every = ("z", "x", "y", "c")
    return jax.shard_map(
        on_device,
        mesh=split,
        in_specs=(P("z", tm, None), P(tm, "z"), P(tm), P()),
        out_specs=(P(every, None), P(every)),
        check_vma=False,
    )
```

profile of v0, /device:TPU:1, one launch (start us, length us, event | category | flops | bytes accessed | tf_op | source)
XLA Modules:
  0.0 36.3 jit_solution(15044967282532746936)
XLA Ops:
  0.6 3.3 %local_sums.1 = (f32[520,128]{1,0:T(8,128)S(1)}, f32[520,128]{1,0:T(8,128)S(1)}) custom-call(bf16[512,2,2048]{2,1,0:T(2,128)(2,1)} %values_hbm.1, f32[2,512]{1,0:T(2,128)} %hazard_hbm.1, f32[1,2]{1,0:T(1,128)} %bitcast.5, s32[1,2048]{1,0:T(1,128)} %bitcast.4), custom_call_target="tpu_custom_call" | custom-call | flops 1073741824 | bytes 5242880 | tf_op jit(solution)/shard_map/local_sums/pallas_call | solution.py:115
  3.9 3.3 %collective-permute-start = (f32[520,128]{1,0:T(8,128)S(1)}, f32[520,128]{1,0:T(8,128)S(1)}, u32[]{:S(2)}, u32[]{:S(2)}) collective-permute-start(f32[520,128]{1,0:T(8,128)S(1)} %get-tuple-element.9), channel_id=1, source_target_pairs={{0,1},{1,0},{2,3},{3,2},{4,5},{5,4},{6,7},{7,6},{8,9},{9,8},{10,11... | collective-permute-start | bytes 798728 | tf_op jit(solution)/shard_map/ppermute | solution.py:250
  7.2 1.2 %collective-permute-done.got_ref = f32[520,128]{1,0:T(8,128)S(1)} collective-permute-done((f32[520,128]{1,0:T(8,128)S(1)}, f32[520,128]{1,0:T(8,128)S(1)}, u32[]{:S(2)}, u32[]{:S(2)}) %collective-permute-start) | collective-permute-done | bytes 266272 | tf_op jit(solution)/shard_map/ppermute | solution.py:250
  8.4 0.3 packed.1
  8.7 12.8 %all_to_all.10.arrived_ref = f32[16,34,2,128]{3,2,1,0:T(2,128)S(1)} all-to-all(f32[16,34,2,128]{3,2,1,0:T(2,128)S(1)} %packed.1), channel_id=1, replica_groups={{20,22,16,18,28,30,24,26,4,6,0,2,12,14,8,10},{21,23,17,19,29,31,25,27,5..., dimensions={0} | all-to-all | bytes 1114112 | tf_op jit(solution)/shard_map/all_to_all | solution.py:252
  21.5 0.1 set_parts.1
  21.6 13.8 %all_to_all.11.parts_ref = f32[16,1,128]{2,1,0:T(1,128)S(1)} all-to-all(f32[16,1,128]{2,1,0:T(1,128)S(1)} %get-tuple-element.11), channel_id=1, replica_groups={{128,160,192,224,0,32,64,96,129,161,193,225,1,33,65,97},{130,162,194,22..., dimensions={0} | all-to-all | bytes 16384 | tf_op jit(solution)/shard_map/all_to_all | solution.py:257
  35.4 0.8 %last_sums.1 = (f32[16,256]{1,0:T(8,128)}, f32[1,128]{1,0:T(1,128)}) custom-call(f32[16,34,2,128]{3,2,1,0:T(2,128)S(1)} %all_to_all.10.arrived_ref, f32[2,16,128]{2,1,0:T(8,128)S(1)} %get-tuple-element.10.earlier_ref, f32[16,1,128]{2,1,0:T(1,128)S(1)} %all_to_all.11.parts_ref), custom_call_target="tpu_custom_call" | custom-call | flops 1000000 | bytes 524288 | tf_op jit(solution)/shard_map/last_sums/pallas_call | solution.py:233
Async XLA Ops:
  3.9 4.5 %collective-permute-start = (f32[520,128]{1,0:T(8,128)S(1)}, f32[520,128]{1,0:T(8,128)S(1)}, u32[]{:S(2)}, u32[]{:S(2)}) collective-permute-start(f32[520,128]{1,0:T(8,128)S(1)} %get-tuple-element.9), channel_id=1, source_target_pairs={{0,1},{1,0},{2,3},{3,2},{4,5},{5,4},{6,7},{7,6},{8,9},{9,8},{10,11... | collective-permute-start | bytes 798728 | tf_op jit(solution)/shard_map/ppermute | solution.py:250
where the time goes:
time: 36.5 us; the launch traced here: 36.3 us
  blocking collectives  26.6 us (73%)
  Pallas kernels  4.49 us (12%)
  starting transfers between devices  3.33 us (9%)
  waiting for transfers between devices  1.17 us (3%)
  between operations  0.65 us (2%)
    all_to_all x1, blocking collectives, on_device(): lax.all_to_all(parts, ('c', 'z'), 0, 0, tiled=True, axis_index_groups=[or...  13.8 us
    all_to_all x1, blocking collectives, on_device(): lax.all_to_all(packed(keep, got), ('x', 'y'), 0, 0, tiled=True, axis_inde...  12.8 us
    ppermute x1, starting transfers between devices, on_device(): got = lax.ppermute(give, 'c', [(0, 1), (1, 0)])  3.33 us
    pallas_call x1, Pallas kernels, local_sums(): pl.pallas_call(net_kernel, out_shape=(HALF, HALF), in_specs=[ANY, ANY, AN...  3.27 us
    ppermute x1, waiting for transfers between devices, on_device(): got = lax.ppermute(give, 'c', [(0, 1), (1, 0)])  1.17 us
    pallas_call x1, Pallas kernels, last_sums(): pl.pallas_call(last_kernel, out_shape=(jax.ShapeDtypeStruct((16, SETS), j...  0.83 us
  transfers between devices with their start and end apart: 1, of which 1 were waited for; matrix products, arithmetic and copies ran while one was open for 0% of the time, Pallas kernels for 0%

commit v1 on v0

--- a/solution.py
+++ b/solution.py
@@ -190,7 +190,7 @@
             total[part] = total[part] + row * rows_ref[at : at + 16, :]
     sums = jnp.sum(total[0] + total[1], axis=1, keepdims=True) * (1.0 / PATHS)
     sums = jnp.broadcast_to(sums, (16, LANES))
-    order = [sums[4:8], sums[0:4], sums[12:16], sums[8:12]]
+    order = [sums[5:8], sums[0:5], sums[13:16], sums[8:13]]
     parts_ref[...] = jnp.concatenate(order, axis=0)[:, None, :]
 
 
@@ -253,7 +253,7 @@
         packed(keep, got), ("x", "y"), 0, 0, tiled=True, axis_index_groups=[chips]
     )
     earlier, parts = set_parts(arrived)
-    order = [core * 8 + (z + 4) % 8 for core in range(2) for z in range(8)]
+    order = [core * 8 + (z + 5) % 8 for core in range(2) for z in range(8)]
     parts = lax.all_to_all(parts, ("c", "z"), 0, 0, tiled=True, axis_index_groups=[order])
     pathwise, sets = last_sums(arrived, earlier, parts)
     return pathwise, sets[0, 0:1]

time: 36.5 us -> 36.5 us (level)
  no operation moved by 1% of the time
where the time goes in v1:
time: 36.5 us; the launch traced here: 36.3 us
  blocking collectives  26.7 us (73%)
  Pallas kernels  4.49 us (12%)
  starting transfers between devices  3.33 us (9%)
  waiting for transfers between devices  1.17 us (3%)
  between operations  0.65 us (2%)
    all_to_all x1, blocking collectives, on_device(): lax.all_to_all(parts, ('c', 'z'), 0, 0, tiled=True, axis_index_groups=[or...  13.8 us
    all_to_all x1, blocking collectives, on_device(): lax.all_to_all(packed(keep, got), ('x', 'y'), 0, 0, tiled=True, axis_inde...  12.8 us
    ppermute x1, starting transfers between devices, on_device(): got = lax.ppermute(give, 'c', [(0, 1), (1, 0)])  3.33 us
    pallas_call x1, Pallas kernels, local_sums(): pl.pallas_call(net_kernel, out_shape=(HALF, HALF), in_specs=[ANY, ANY, AN...  3.27 us
    ppermute x1, waiting for transfers between devices, on_device(): got = lax.ppermute(give, 'c', [(0, 1), (1, 0)])  1.17 us
    pallas_call x1, Pallas kernels, last_sums(): pl.pallas_call(last_kernel, out_shape=(jax.ShapeDtypeStruct((16, SETS), j...  0.83 us
  transfers between devices with their start and end apart: 1, of which 1 were waited for; matrix products, arithmetic and copies ran while one was open for 0% of the time, Pallas kernels for 0%

profile of v1, /device:TPU:1, one launch (start us, length us, event | category | flops | bytes accessed | tf_op | source)
XLA Modules:
  0.0 36.3 jit_solution(9458775279374016183)
XLA Ops:
  0.6 3.3 %local_sums.1 = (f32[520,128]{1,0:T(8,128)S(1)}, f32[520,128]{1,0:T(8,128)S(1)}) custom-call(bf16[512,2,2048]{2,1,0:T(2,128)(2,1)} %values_hbm.1, f32[2,512]{1,0:T(2,128)} %hazard_hbm.1, f32[1,2]{1,0:T(1,128)} %bitcast.5, s32[1,2048]{1,0:T(1,128)} %bitcast.4), custom_call_target="tpu_custom_call" | custom-call | flops 1073741824 | bytes 5242880 | tf_op jit(solution)/shard_map/local_sums/pallas_call | solution.py:115
  3.9 3.3 %collective-permute-start = (f32[520,128]{1,0:T(8,128)S(1)}, f32[520,128]{1,0:T(8,128)S(1)}, u32[]{:S(2)}, u32[]{:S(2)}) collective-permute-start(f32[520,128]{1,0:T(8,128)S(1)} %get-tuple-element.9), channel_id=1, source_target_pairs={{0,1},{1,0},{2,3},{3,2},{4,5},{5,4},{6,7},{7,6},{8,9},{9,8},{10,11... | collective-permute-start | bytes 798728 | tf_op jit(solution)/shard_map/ppermute | solution.py:250
  7.2 1.2 %collective-permute-done.got_ref = f32[520,128]{1,0:T(8,128)S(1)} collective-permute-done((f32[520,128]{1,0:T(8,128)S(1)}, f32[520,128]{1,0:T(8,128)S(1)}, u32[]{:S(2)}, u32[]{:S(2)}) %collective-permute-start) | collective-permute-done | bytes 266272 | tf_op jit(solution)/shard_map/ppermute | solution.py:250
  8.4 0.3 packed.1
  8.7 12.8 %all_to_all.10.arrived_ref = f32[16,34,2,128]{3,2,1,0:T(2,128)S(1)} all-to-all(f32[16,34,2,128]{3,2,1,0:T(2,128)S(1)} %packed.1), channel_id=1, replica_groups={{20,22,16,18,28,30,24,26,4,6,0,2,12,14,8,10},{21,23,17,19,29,31,25,27,5..., dimensions={0} | all-to-all | bytes 1114112 | tf_op jit(solution)/shard_map/all_to_all | solution.py:252
  21.5 0.1 set_parts.1
  21.6 13.8 %all_to_all.11.parts_ref = f32[16,1,128]{2,1,0:T(1,128)S(1)} all-to-all(f32[16,1,128]{2,1,0:T(1,128)S(1)} %get-tuple-element.11), channel_id=1, replica_groups={{160,192,224,0,32,64,96,128,161,193,225,1,33,65,97,129},{162,194,226,2,..., dimensions={0} | all-to-all | bytes 16384 | tf_op jit(solution)/shard_map/all_to_all | solution.py:257
  35.5 0.8 %last_sums.1 = (f32[16,256]{1,0:T(8,128)}, f32[1,128]{1,0:T(1,128)}) custom-call(f32[16,34,2,128]{3,2,1,0:T(2,128)S(1)} %all_to_all.10.arrived_ref, f32[2,16,128]{2,1,0:T(8,128)S(1)} %get-tuple-element.10.earlier_ref, f32[16,1,128]{2,1,0:T(1,128)S(1)} %all_to_all.11.parts_ref), custom_call_target="tpu_custom_call" | custom-call | flops 1000000 | bytes 524288 | tf_op jit(solution)/shard_map/last_sums/pallas_call | solution.py:233
Async XLA Ops:
  3.9 4.5 %collective-permute-start = (f32[520,128]{1,0:T(8,128)S(1)}, f32[520,128]{1,0:T(8,128)S(1)}, u32[]{:S(2)}, u32[]{:S(2)}) collective-permute-start(f32[520,128]{1,0:T(8,128)S(1)} %get-tuple-element.9), channel_id=1, source_target_pairs={{0,1},{1,0},{2,3},{3,2},{4,5},{5,4},{6,7},{7,6},{8,9},{9,8},{10,11... | collective-permute-start | bytes 798728 | tf_op jit(solution)/shard_map/ppermute | solution.py:250
